TPU v7x, 32 devices: a whole 2x2x4 slice. The times are simulated.
32 devices in a mesh: blk: 8 (over z, core), fsdp: 4 (over y, x).
Axes of the slice: x: 2, y: 2, z: 4, core: 2. Of those that a mesh axis runs over, the one named last changes fastest.
Arguments:
- context: bfloat16 [8, 512, 2048], P('blk', 'fsdp'), may hold values from -6 to 6
- hidden: bfloat16 [8, 512, 4096], P('blk', 'fsdp'), may hold values from -6 to 6
- cotangent: bfloat16 [8, 512, 4096], P('blk', 'fsdp'), may hold values from -6 to 6
- gain: float32 [8, 4096], P('blk'), may hold values from 0.3 to 3
- weight: bfloat16 [8, 2048, 4096], P('blk', None, 'fsdp'), may hold values from -6 to 6
- step_counts: int32 [8], P('blk'), may hold values from 1 to 256
Outputs:
- new_weight: bfloat16 [8, 2048, 4096], P('blk', None, 'fsdp')
All inputs are finite; a program needn't handle non-finite values.
Results may differ from a plain program's by a relative error of at most 0.0038.
Values may be sent and summed in bfloat16 or wider, within the bound.
A program may use at most 64 MiB of HBM per device.

v0:
```python
import math
import jax
import jax.numpy as jnp
from jax import lax
from jax.sharding import PartitionSpec as P


def passed_along(block, axis, distance):
    devices = range(lax.axis_size(axis))
    route = [((i - distance) % len(devices), i) for i in devices]
    return lax.ppermute(block, axis, route)


def body(context, hidden, cotangent, gain, weight, step_counts):
    inputs = context[0]
    own = weight[0]
    width = inputs.shape[1]
    group = lax.axis_size("fsdp")
    rows = inputs.shape[0] * group
    scale = 1.0 / math.sqrt(width)
    rate = 0.5 * math.sqrt(width / rows)
    counts_wire = step_counts.astype(jnp.bfloat16)
    low_weight, low_count = passed_along((weight, counts_wire), "blk", 1)
    high_weight, high_count = passed_along((weight, counts_wire), "blk", -1)
    gathered = lax.all_gather(inputs, "fsdp", axis=0, tiled=True)
    branch = (jnp.dot(gathered, own, preferred_element_type=jnp.float32) * scale).astype(
        jnp.bfloat16
    )
    branch_rows = lax.all_to_all(branch, "fsdp", split_axis=0, concat_axis=1, tiled=True)
    residual_out = hidden[0].astype(jnp.float32) + branch_rows.astype(jnp.float32)
    inv_rms = lax.rsqrt(jnp.mean(residual_out * residual_out, axis=-1, keepdims=True) + 1e-05)
    scaled = gain[0][None, :] * cotangent[0].astype(jnp.float32)
    cross = jnp.mean(scaled * residual_out, axis=-1, keepdims=True)
    grad_rows = (inv_rms * scaled - residual_out * inv_rms**3 * cross).astype(jnp.bfloat16)
    out_grad = lax.all_to_all(grad_rows, "fsdp", split_axis=1, concat_axis=0, tiled=True)
    grad = (
        lax.dot_general(
            gathered, out_grad, (((0,), (0,)), ((), ())), preferred_element_type=jnp.float32
        )
        * scale
    )
    lower_c = low_count.astype(jnp.float32)[0]
    own_c = step_counts.astype(jnp.float32)[0]
    upper_c = high_count.astype(jnp.float32)[0]
    total = lower_c + own_c + upper_c
    mixed = (
        lower_c * low_weight[0].astype(jnp.float32)
        + own_c * own.astype(jnp.float32)
        + upper_c * high_weight[0].astype(jnp.float32)
    ) / total
    return (mixed - rate * grad).astype(jnp.bfloat16)[None]


def solution(mesh):
    return jax.shard_map(
        body,
        mesh=mesh,
        in_specs=(
            P("blk", "fsdp", None),
            P("blk", "fsdp", None),
            P("blk", "fsdp", None),
            P("blk", None),
            P("blk", None, "fsdp"),
            P("blk"),
        ),
        out_specs=P("blk", None, "fsdp"),
        check_vma=False,
    )
```

profile of v0, /device:TPU:0, one launch (start us, length us, event | category | flops | bytes accessed | tf_op | source)
XLA Modules:
  0.0 136.4 jit_solution(17001051425902305718)
XLA Ops:
  6.5 0.7 all-gather.3.cloned.1.call-update
  7.3 6.4 %copy.7 = bf16[1,2048,1024]{1,2,0:T(8,128)(2,1)} copy(bf16[1,2048,1024]{2,1,0:T(8,128)(2,1)} %param.10) | data formatting | bytes 8388608 | tf_op args[4]
  13.7 4.5 %collective-permute-start.3 = (bf16[1,2048,1024]{1,2,0:T(8,128)(2,1)}, bf16[1,2048,1024]{1,2,0:T(8,128)(2,1)}, u32[]{:S(2)}, u32[]{:S(2)}) collective-permute-start(bf16[1,2048,1024]{1,2,0:T(8,128)(2,1)} %copy.7), channel_id=1, source_target_pairs={{4,0},{8,4},{12,8},{16,12},{20,16},{24,20},{28,24},{0,28},{5,1},{9... | collective-permute-start | bytes 12582920 | tf_op jit(solution)/shard_map/ppermute | solution.py:11
  18.2 29.1 %all-gather.3.cloned.1.call-done = bf16[1,512,2048]{2,1,0:T(8,128)(2,1)} async-done(((bf16[1,128,2048]{2,1,0:T(8,128)(2,1)}), bf16[1,512,2048]{2,1,0:T(8,128)(2,1)}) %all-gather.3.cloned.1.call-update) | async-done | bytes 2097168 | tf_op jit(solution)/shard_map/all_gather | solution.py:25
  47.2 6.2 %multiply_convert_fusion = bf16[512,1024]{1,0:T(8,128)(2,1)} fusion(bf16[1,2048,1024]{2,1,0:T(8,128)(2,1)} %param.10, bf16[1,512,2048]{2,1,0:T(8,128)(2,1)} %all-gather.3.cloned.1.call-done), kind=kOutput, calls=%fused_computation.25 | convolution fusion | flops 2148532224 | bytes 7340032 | tf_op jit(solution)/shard_map/dot_general | solution.py:26
  53.4 3.6 %all-to-all-start = ((bf16[4,128,1024]{2,1,0:T(8,128)(2,1)}), bf16[4,128,1024]{2,1,0:T(8,128)(2,1)S(1)}, u32[]{:S(2)}, u32[]{:S(2)}) async-start(bf16[4,128,1024]{2,1,0:T(8,128)(2,1)} %bitcast.10), calls=%async_computation | async-start | bytes 2097152 | tf_op jit(solution)/shard_map/all_to_all | solution.py:29
  57.1 0.5 broadcast.54
  57.6 0.6 reduce.3
  58.2 2.7 %reshape.67 = f32[128,4,1024]{2,1,0:T(4,128)S(1)} reshape(bf16[1,128,4096]{2,1,0:T(8,128)(2,1)} %param.7) | data formatting | bytes 3145728 | tf_op jit(solution)/shard_map/convert_element_type | solution.py:30
  61.0 3.7 %reshape.66 = f32[128,4,1024]{2,1,0:T(4,128)} reshape(bf16[1,128,4096]{2,1,0:T(8,128)(2,1)} %param.8) | data formatting | bytes 3145728 | tf_op jit(solution)/shard_map/convert_element_type | solution.py:32
  64.7 6.3 %all-to-all-done = bf16[4,128,1024]{2,1,0:T(8,128)(2,1)S(1)} async-done(((bf16[4,128,1024]{2,1,0:T(8,128)(2,1)}), bf16[4,128,1024]{2,1,0:T(8,128)(2,1)S(1)}, u32[]{:S(2)}, u32[]{:S(2)}) %all-to-all-start) | async-done | bytes 1048608 | tf_op jit(solution)/shard_map/all_to_all | solution.py:29
  71.0 0.2 convert_bitcast_fusion
  71.2 0.2 copy.14
  71.5 1.0 copy-done.1
  72.5 0.3 copy-done.2
  72.8 0.7 multiply_reduce_fusion
  73.5 0.9 copy-done
  74.4 3.8 %fusion.9 = bf16[128,4,1024]{2,0,1:T(8,128)(2,1)} fusion(bf16[4,128,1024]{2,1,0:T(8,128)(2,1)S(1)} %all-to-all-done, f32[128,4,1024]{2,1,0:T(4,128)S(1)} %reshape.67, f32[128,4,1024]{2,1,0:T(4,128)S(1)} %copy-done, f32[128]{0:T(128)S(1)} %get-tuple-element.9, f32[128]{0:T(128)S(1)} %get-tuple-element.8, f32[4,1024]{1,0:T(4,128)S(1)} %mul.101, ...), kind=kLoop, calls=%fused_computation.14 | loop fusion | flops 4194304 | bytes 6309376 | tf_op jit(solution)/shard_map/convert_element_type | solution.py:34
  78.1 3.6 %all-to-all-start.1 = ((bf16[128,4,1024]{2,0,1:T(8,128)(2,1)}), bf16[128,4,1024]{2,0,1:T(8,128)(2,1)S(1)}, u32[]{:S(2)}, u32[]{:S(2)}) async-start(bf16[128,4,1024]{2,0,1:T(8,128)(2,1)} %fusion.9), calls=%async_computation.1 | async-start | bytes 2097152 | tf_op jit(solution)/shard_map/all_to_all | solution.py:35
  82.4 25.0 %collective-permute-start.2 = (bf16[1]{0:T(256)(128)(2,1)}, bf16[1]{0:T(256)(128)(2,1)}, u32[]{:S(2)}, u32[]{:S(2)}) collective-permute-start(bf16[1]{0:T(256)(128)(2,1)} %convert_element_type.66), channel_id=1, source_target_pairs={{4,0},{8,4},{12,8},{16,12},{20,16},{24,20},{28,24},{0,28},{5,1},{9... | collective-permute-start | bytes 14 | tf_op jit(solution)/shard_map/ppermute | solution.py:11
  107.5 0.8 collective-permute-start
  108.9 3.3 %collective-permute-done = bf16[1]{0:T(256)(128)(2,1)} collective-permute-done((bf16[1]{0:T(256)(128)(2,1)}, bf16[1]{0:T(256)(128)(2,1)}, u32[]{:S(2)}, u32[]{:S(2)}) %collective-permute-start) | collective-permute-done | bytes 34 | tf_op jit(solution)/shard_map/ppermute | solution.py:11
  114.2 9.0 %fusion.4 = bf16[1,2048,1024]{1,2,0:T(8,128)(2,1)} fusion(f32[]{:T(128)S(6)} %add.35, bf16[1,2048,1024]{1,2,0:T(8,128)(2,1)} %collective-permute-done.3, f32[]{:T(128)S(6)} %convert.10, bf16[1,2048,1024]{1,2,0:T(8,128)(2,1)} %copy.7, f32[]{:T(128)} %bitcast.2, bf16[1,2048,1024]{1,2,0:T(8,128)(2,1)} %collective-permute-done.1, f32[]{:T(128)S(6)} %convert.9, ...), kind=kOutput, calls=%fused_computation.7 | convolution fusion | flops 2172649472 | bytes 19922960 | tf_op jit(solution)/shard_map/dot_general | solution.py:37
  123.2 6.4 %copy.13 = bf16[1,2048,1024]{2,1,0:T(8,128)(2,1)} copy(bf16[1,2048,1024]{1,2,0:T(8,128)(2,1)} %fusion.4) | data formatting | bytes 8388608 | tf_op jit(solution)/shard_map/broadcast_in_dim | solution.py:51
  (15 shorter events, 0.1 us)
Async XLA Ops:
  6.5 40.7 %all-gather.3.cloned.1.call-start = ((), (), s32[]{:S(2)}) async-start(), calls=%async_computation.2 | async-start | bytes 2621440 | tf_op jit(solution)/shard_map/all_gather | solution.py:25
  13.7 100.5 %collective-permute-start.3 = (bf16[1,2048,1024]{1,2,0:T(8,128)(2,1)}, bf16[1,2048,1024]{1,2,0:T(8,128)(2,1)}, u32[]{:S(2)}, u32[]{:S(2)}) collective-permute-start(bf16[1,2048,1024]{1,2,0:T(8,128)(2,1)} %copy.7), channel_id=1, source_target_pairs={{4,0},{8,4},{12,8},{16,12},{20,16},{24,20},{28,24},{0,28},{5,1},{9... | collective-permute-start | bytes 12582920 | tf_op jit(solution)/shard_map/ppermute | solution.py:11
  18.2 96.0 %collective-permute-start.1 = (bf16[1,2048,1024]{1,2,0:T(8,128)(2,1)}, bf16[1,2048,1024]{1,2,0:T(8,128)(2,1)}, u32[]{:S(2)}, u32[]{:S(2)}) collective-permute-start(bf16[1,2048,1024]{1,2,0:T(8,128)(2,1)} %copy.7), channel_id=1, source_target_pairs={{28,0},{0,4},{4,8},{8,12},{12,16},{16,20},{20,24},{24,28},{29,1},{... | collective-permute-start | bytes 12582920 | tf_op jit(solution)/shard_map/ppermute | solution.py:11
  53.4 4.1 %copy-start.3 = (f32[1,4096]{1,0:T(1,128)S(1)}, f32[1,4096]{1,0:T(1,128)}, u32[]{:S(2)}) copy-start(f32[1,4096]{1,0:T(1,128)} %param.9) | copy-start | bytes 49156
  53.4 17.5 %all-to-all-start = ((bf16[4,128,1024]{2,1,0:T(8,128)(2,1)}), bf16[4,128,1024]{2,1,0:T(8,128)(2,1)S(1)}, u32[]{:S(2)}, u32[]{:S(2)}) async-start(bf16[4,128,1024]{2,1,0:T(8,128)(2,1)} %bitcast.10), calls=%async_computation | async-start | bytes 2097152 | tf_op jit(solution)/shard_map/all_to_all | solution.py:29
  71.2 1.2 copy-start.1
  71.2 1.5 %copy-start.2 = (bf16[1,128,4096]{2,1,0:T(8,128)(2,1)S(1)}, bf16[1,128,4096]{2,1,0:T(8,128)(2,1)}, u32[]{:S(2)}) copy-start(bf16[1,128,4096]{2,1,0:T(8,128)(2,1)} %param.8) | copy-start | bytes 3145732
  72.8 1.6 %copy-start = (f32[128,4,1024]{2,1,0:T(4,128)S(1)}, f32[128,4,1024]{2,1,0:T(4,128)}, u32[]{:S(2)}) copy-start(f32[128,4,1024]{2,1,0:T(4,128)} %reshape.66) | copy-start | bytes 6291460
  78.1 36.1 %copy-start.4 = (bf16[1,512,2048]{2,1,0:T(8,128)(2,1)S(1)}, bf16[1,512,2048]{2,1,0:T(8,128)(2,1)}, u32[]{:S(2)}) copy-start(bf16[1,512,2048]{2,1,0:T(8,128)(2,1)} %all-gather.3.cloned.1.call-done) | copy-start | bytes 6291460
  78.1 36.0 %all-to-all-start.1 = ((bf16[128,4,1024]{2,0,1:T(8,128)(2,1)}), bf16[128,4,1024]{2,0,1:T(8,128)(2,1)S(1)}, u32[]{:S(2)}, u32[]{:S(2)}) async-start(bf16[128,4,1024]{2,0,1:T(8,128)(2,1)} %fusion.9), calls=%async_computation.1 | async-start | bytes 2097152 | tf_op jit(solution)/shard_map/all_to_all | solution.py:35
  82.4 25.9 %collective-permute-start.2 = (bf16[1]{0:T(256)(128)(2,1)}, bf16[1]{0:T(256)(128)(2,1)}, u32[]{:S(2)}, u32[]{:S(2)}) collective-permute-start(bf16[1]{0:T(256)(128)(2,1)} %convert_element_type.66), channel_id=1, source_target_pairs={{4,0},{8,4},{12,8},{16,12},{20,16},{24,20},{28,24},{0,28},{5,1},{9... | collective-permute-start | bytes 14 | tf_op jit(solution)/shard_map/ppermute | solution.py:11
  107.5 4.7 %collective-permute-start = (bf16[1]{0:T(256)(128)(2,1)}, bf16[1]{0:T(256)(128)(2,1)}, u32[]{:S(2)}, u32[]{:S(2)}) collective-permute-start(bf16[1]{0:T(256)(128)(2,1)} %convert_element_type.66), channel_id=1, source_target_pairs={{28,0},{0,4},{4,8},{8,12},{12,16},{16,20},{20,24},{24,28},{29,1},{... | collective-permute-start | bytes 14 | tf_op jit(solution)/shard_map/ppermute | solution.py:11
Sparse Core Ops, SparseCore 0:
  9.2 38.0 all-gather.2
where the time goes:
time: 137 us; the launch traced here: 136 us
  waiting for transfers between devices  39.4 us (29%)
  starting transfers between devices  37.6 us (27%)
  local copies, waits for them, and re-layouts  22.2 us (16%)
  between operations  16.7 us (12%)
  matrix products  15.2 us (11%)
  other arithmetic  5.3 us (4%)
    ppermute x4, starting transfers between devices, passed_along(): return lax.ppermute(block, axis, route)  30.3 us
    all_gather x1, waiting for transfers between devices, body(): gathered = lax.all_gather(inputs, 'fsdp', axis=0, tiled=True)  29.1 us
    unnamed x12, local copies, waits for them, and re-layouts  9.12 us
    dot_general x1, matrix products, body(): lax.dot_general(gathered, out_grad, (((0,), (0,)), ((), ())), preferred_e...  8.97 us
    broadcast_in_dim x1, local copies, waits for them, and re-layouts, body(): return (mixed - rate * grad).astype(jnp.bfloat16)[None]  6.39 us
    all_to_all x1, waiting for transfers between devices, body(): lax.all_to_all(branch, 'fsdp', split_axis=0, concat_axis=1, tiled=True)  6.27 us
    dot_general x1, matrix products, body(): jnp.dot(gathered, own, preferred_element_type=jnp.float32) * scale  6.19 us
    convert_element_type x1, other arithmetic, body(): (inv_rms * scaled - residual_out * inv_rms ** 3 * cross).astype(jnp.bfloa...  3.78 us
  transfers between devices with their start and end apart: 7, of which 3 were waited for; matrix products, arithmetic and copies ran while one was open for 18% of the time, Pallas kernels for 0%

commit v1 on v0

--- a/solution.py
+++ b/solution.py
@@ -22,7 +22,15 @@
     counts_wire = step_counts.astype(jnp.bfloat16)
     low_weight, low_count = passed_along((weight, counts_wire), "blk", 1)
     high_weight, high_count = passed_along((weight, counts_wire), "blk", -1)
-    gathered = lax.all_gather(inputs, "fsdp", axis=0, tiled=True)
+    ways, here = (lax.axis_size("fsdp"), lax.axis_index("fsdp"))
+    grown, reach = (inputs, 1)
+    while reach < ways:
+        theirs = lax.ppermute(grown, "fsdp", [(d, d ^ reach) for d in range(ways)])
+        mine_first = jnp.concatenate([grown, theirs], axis=0)
+        theirs_first = jnp.concatenate([theirs, grown], axis=0)
+        grown = jnp.where(here & reach == 0, mine_first, theirs_first)
+        reach = 2 * reach
+    gathered = grown
     branch = (jnp.dot(gathered, own, preferred_element_type=jnp.float32) * scale).astype(
         jnp.bfloat16
     )

time: 137 us -> 127 us (0.927)
  starting transfers between devices: 37.6 us -> 52.9 us
  between operations: 16.7 us -> 3.33 us
  local copies, waits for them, and re-layouts: 22.2 us -> 9.42 us
  other arithmetic: 5.3 us -> 6.96 us
    ppermute x0 -> x2, waiting for transfers between devices: none -> 31.2 us  [body(): theirs = lax.ppermute(grown, 'fsdp', [(d, d ^ reach) for d in range(ways)])]
    all_gather x1 -> x0, waiting for transfers between devices: 29.1 us -> none  [body(): gathered = lax.all_gather(inputs, 'fsdp', axis=0, tiled=True)]
    ppermute x4, starting transfers between devices: 30.3 us -> 40.7 us  [passed_along(): return lax.ppermute(block, axis, route)]
    unnamed x12 -> x17, local copies, waits for them, and re-layouts: 9.12 us -> 2.72 us
    broadcast_in_dim x1 -> x0, local copies, waits for them, and re-layouts: 6.39 us -> none  [body(): return (mixed - rate * grad).astype(jnp.bfloat16)[None]]
    ppermute x0 -> x2, starting transfers between devices: none -> 4.78 us  [body(): theirs = lax.ppermute(grown, 'fsdp', [(d, d ^ reach) for d in range(ways)])]
    select_n x0 -> x1, other arithmetic: none -> 1.59 us  [body(): grown = jnp.where(here & reach == 0, mine_first, theirs_first)]
    all_to_all x1, waiting for transfers between devices: 6.27 us -> 4.71 us  [body(): lax.all_to_all(branch, 'fsdp', split_axis=0, concat_axis=1, tiled=True)]
  transfers between devices with their start and end apart: 7 -> 8, of which waited for: 3 -> 4; matrix products, arithmetic and copies ran while one was open for 18% -> 15% of each run, Pallas kernels for 0% -> 0%
where the time goes in v1:
time: 127 us
  starting transfers between devices  52.9 us (42%)
  waiting for transfers between devices  39.1 us (31%)
  matrix products  15 us (12%)
  local copies, waits for them, and re-layouts  9.42 us (7%)
  other arithmetic  6.96 us (5%)
  between operations  3.33 us (3%)
    ppermute x4, starting transfers between devices, passed_along(): return lax.ppermute(block, axis, route)  40.7 us
    ppermute x2, waiting for transfers between devices, body(): theirs = lax.ppermute(grown, 'fsdp', [(d, d ^ reach) for d in range(ways)])  31.2 us
    dot_general x1, matrix products, body(): lax.dot_general(gathered, out_grad, (((0,), (0,)), ((), ())), preferred_e...  9.11 us
    dot_general x1, matrix products, body(): jnp.dot(gathered, own, preferred_element_type=jnp.float32) * scale  5.89 us
    ppermute x2, starting transfers between devices, body(): theirs = lax.ppermute(grown, 'fsdp', [(d, d ^ reach) for d in range(ways)])  4.78 us
    all_to_all x1, waiting for transfers between devices, body(): lax.all_to_all(branch, 'fsdp', split_axis=0, concat_axis=1, tiled=True)  4.71 us
    all_to_all x1, starting transfers between devices, body(): lax.all_to_all(branch, 'fsdp', split_axis=0, concat_axis=1, tiled=True)  3.79 us
    convert_element_type x1, other arithmetic, body(): (inv_rms * scaled - residual_out * inv_rms ** 3 * cross).astype(jnp.bfloa...  3.77 us
  transfers between devices with their start and end apart: 8, of which 4 were waited for; matrix products, arithmetic and copies ran while one was open for 15% of the time, Pallas kernels for 0%

profile of v1, /device:TPU:0, one launch (start us, length us, event | category | flops | bytes accessed | tf_op | source)
XLA Modules:
  0.0 126.8 jit_solution(8952814256427994535)
XLA Ops:
  0.0 2.9 %collective-permute-start.4 = (bf16[128,2048]{1,0:T(8,128)(2,1)}, bf16[128,2048]{1,0:T(8,128)(2,1)S(1)}, u32[]{:S(2)}, u32[]{:S(2)}) collective-permute-start(bf16[128,2048]{1,0:T(8,128)(2,1)} %bitcast.67), channel_id=1, source_target_pairs={{0,1},{1,0},{2,3},{3,2},{4,5},{5,4},{6,7},{7,6},{8,9},{9,8},{10,11... | collective-permute-start | bytes 1572872 | tf_op jit(solution)/shard_map/ppermute | solution.py:28
  2.9 12.1 %collective-permute-done.4 = bf16[128,2048]{1,0:T(8,128)(2,1)S(1)} collective-permute-done((bf16[128,2048]{1,0:T(8,128)(2,1)}, bf16[128,2048]{1,0:T(8,128)(2,1)S(1)}, u32[]{:S(2)}, u32[]{:S(2)}) %collective-permute-start.4) | collective-permute-done | bytes 524320 | tf_op jit(solution)/shard_map/ppermute | solution.py:28
  15.1 1.6 %maximum_select_fusion.1 = bf16[256,2048]{1,0:T(8,128)(2,1)S(1)} fusion(bf16[128,2048]{1,0:T(8,128)(2,1)S(1)} %collective-permute-done.4, bf16[128,2048]{1,0:T(8,128)(2,1)} %bitcast.68, pred[]{:T(512)S(6)} %eq.7), kind=kLoop, calls=%fused_computation.24 | loop fusion | flops 4718592 | bytes 2097153 | tf_op jit(solution)/shard_map/jit(_where)/select_n | solution.py:31
  16.7 1.8 %collective-permute-start.5 = (bf16[256,2048]{1,0:T(8,128)(2,1)S(1)}, bf16[256,2048]{1,0:T(8,128)(2,1)S(1)}, u32[]{:S(2)}, u32[]{:S(2)}) collective-permute-start(bf16[256,2048]{1,0:T(8,128)(2,1)S(1)} %maximum_select_fusion.1), channel_id=1, source_target_pairs={{0,2},{1,3},{2,0},{3,1},{4,6},{5,7},{6,4},{7,5},{8,10},{9,11},{10,... | collective-permute-start | bytes 3145736 | tf_op jit(solution)/shard_map/ppermute | solution.py:28
  18.5 3.5 %collective-permute-start.3 = (bf16[1,2048,1024]{2,1,0:T(8,128)(2,1)}, bf16[1,2048,1024]{2,1,0:T(8,128)(2,1)}, u32[]{:S(2)}, u32[]{:S(2)}) collective-permute-start(bf16[1,2048,1024]{2,1,0:T(8,128)(2,1)} %param.10), channel_id=1, source_target_pairs={{4,0},{8,4},{12,8},{16,12},{20,16},{24,20},{28,24},{0,28},{5,1},{9... | collective-permute-start | bytes 12582920 | tf_op jit(solution)/shard_map/ppermute | solution.py:11
  22.1 19.0 %collective-permute-done.5 = bf16[256,2048]{1,0:T(8,128)(2,1)S(1)} collective-permute-done((bf16[256,2048]{1,0:T(8,128)(2,1)S(1)}, bf16[256,2048]{1,0:T(8,128)(2,1)S(1)}, u32[]{:S(2)}, u32[]{:S(2)}) %collective-permute-start.5) | collective-permute-done | bytes 1048608 | tf_op jit(solution)/shard_map/ppermute | solution.py:28
  41.1 5.9 %multiply_convert_fusion = bf16[512,1024]{1,0:T(8,128)(2,1)} fusion(bf16[1,2048,1024]{2,1,0:T(8,128)(2,1)} %param.10, bf16[256,2048]{1,0:T(8,128)(2,1)S(1)} %collective-permute-done.5, bf16[256,2048]{1,0:T(8,128)(2,1)S(1)} %maximum_select_fusion.1, pred[]{:T(512)S(6)} %eq.6), kind=kOutput, calls=%fused_computation.23 | convolution fusion | flops 2157969408 | bytes 7340033 | tf_op jit(solution)/shard_map/dot_general | solution.py:34
  47.0 3.8 %all-to-all-start = ((bf16[4,128,1024]{2,1,0:T(8,128)(2,1)}), bf16[4,128,1024]{2,1,0:T(8,128)(2,1)S(1)}, u32[]{:S(2)}, u32[]{:S(2)}) async-start(bf16[4,128,1024]{2,1,0:T(8,128)(2,1)} %bitcast.10), calls=%async_computation | async-start | bytes 2097152 | tf_op jit(solution)/shard_map/all_to_all | solution.py:37
  50.8 0.5 broadcast.52
  51.3 0.7 reduce.3
  52.0 2.7 %reshape.67 = f32[128,4,1024]{2,1,0:T(4,128)S(1)} reshape(bf16[1,128,4096]{2,1,0:T(8,128)(2,1)} %param.7) | data formatting | bytes 3145728 | tf_op jit(solution)/shard_map/convert_element_type | solution.py:38
  54.7 3.7 %reshape.66 = f32[128,4,1024]{2,1,0:T(4,128)} reshape(bf16[1,128,4096]{2,1,0:T(8,128)(2,1)} %param.8) | data formatting | bytes 3145728 | tf_op jit(solution)/shard_map/convert_element_type | solution.py:40
  58.4 4.7 %all-to-all-done = bf16[4,128,1024]{2,1,0:T(8,128)(2,1)S(1)} async-done(((bf16[4,128,1024]{2,1,0:T(8,128)(2,1)}), bf16[4,128,1024]{2,1,0:T(8,128)(2,1)S(1)}, u32[]{:S(2)}, u32[]{:S(2)}) %all-to-all-start) | async-done | bytes 1048608 | tf_op jit(solution)/shard_map/all_to_all | solution.py:37
  63.4 0.2 copy.10
  63.7 1.0 copy-done.1
  64.6 0.3 copy-done.2
  64.9 0.7 multiply_reduce_fusion
  65.6 0.9 copy-done
  66.5 3.8 %fusion.10 = bf16[128,4,1024]{2,0,1:T(8,128)(2,1)} fusion(bf16[4,128,1024]{2,1,0:T(8,128)(2,1)S(1)} %all-to-all-done, f32[128,4,1024]{2,1,0:T(4,128)S(1)} %reshape.67, f32[128,4,1024]{2,1,0:T(4,128)S(1)} %copy-done, f32[128]{0:T(128)S(1)} %get-tuple-element.9, f32[128]{0:T(128)S(1)} %get-tuple-element.8, f32[4,1024]{1,0:T(4,128)S(1)} %mul.98, ...), kind=kLoop, calls=%fused_computation.14 | loop fusion | flops 4194304 | bytes 6309376 | tf_op jit(solution)/shard_map/convert_element_type | solution.py:42
  70.3 3.6 %all-to-all-start.1 = ((bf16[128,4,1024]{2,0,1:T(8,128)(2,1)}), bf16[128,4,1024]{2,0,1:T(8,128)(2,1)S(1)}, u32[]{:S(2)}, u32[]{:S(2)}) async-start(bf16[128,4,1024]{2,0,1:T(8,128)(2,1)} %fusion.10), calls=%async_computation.1 | async-start | bytes 2097152 | tf_op jit(solution)/shard_map/all_to_all | solution.py:43
  74.6 36.2 %collective-permute-start.2 = (bf16[1]{0:T(256)(128)(2,1)}, bf16[1]{0:T(256)(128)(2,1)}, u32[]{:S(2)}, u32[]{:S(2)}) collective-permute-start(bf16[1]{0:T(256)(128)(2,1)} %convert_element_type.66), channel_id=1, source_target_pairs={{4,0},{8,4},{12,8},{16,12},{20,16},{24,20},{28,24},{0,28},{5,1},{9... | collective-permute-start | bytes 14 | tf_op jit(solution)/shard_map/ppermute | solution.py:11
  110.8 1.0 collective-permute-start
  112.4 3.3 %collective-permute-done = bf16[1]{0:T(256)(128)(2,1)} collective-permute-done((bf16[1]{0:T(256)(128)(2,1)}, bf16[1]{0:T(256)(128)(2,1)}, u32[]{:S(2)}, u32[]{:S(2)}) %collective-permute-start) | collective-permute-done | bytes 34 | tf_op jit(solution)/shard_map/ppermute | solution.py:11
  117.7 9.1 %fusion.5 = bf16[1,2048,1024]{2,1,0:T(8,128)(2,1)} fusion(f32[]{:T(128)S(6)} %add.35, bf16[1,2048,1024]{2,1,0:T(8,128)(2,1)} %collective-permute-done.3, f32[]{:T(128)S(6)} %convert.10, bf16[1,2048,1024]{2,1,0:T(8,128)(2,1)} %param.10, f32[]{:T(128)} %bitcast.2, bf16[1,2048,1024]{2,1,0:T(8,128)(2,1)} %collective-permute-done.1, f32[]{:T(128)S(6)} %convert.9, ...), kind=kOutput, calls=%fused_computation.7 | convolution fusion | flops 2182086656 | bytes 19922960 | tf_op jit(solution)/shard_map/dot_general | solution.py:45
  (21 shorter events, 0.3 us)
Async XLA Ops:
  0.0 15.1 %collective-permute-start.4 = (bf16[128,2048]{1,0:T(8,128)(2,1)}, bf16[128,2048]{1,0:T(8,128)(2,1)S(1)}, u32[]{:S(2)}, u32[]{:S(2)}) collective-permute-start(bf16[128,2048]{1,0:T(8,128)(2,1)} %bitcast.67), channel_id=1, source_target_pairs={{0,1},{1,0},{2,3},{3,2},{4,5},{5,4},{6,7},{7,6},{8,9},{9,8},{10,11... | collective-permute-start | bytes 1572872 | tf_op jit(solution)/shard_map/ppermute | solution.py:28
  16.7 30.3 %copy-start.3 = (bf16[256,2048]{1,0:T(8,128)(2,1)}, bf16[256,2048]{1,0:T(8,128)(2,1)S(1)}, u32[]{:S(2)}) copy-start(bf16[256,2048]{1,0:T(8,128)(2,1)S(1)} %maximum_select_fusion.1) | copy-start | bytes 3145732
  16.7 24.4 %collective-permute-start.5 = (bf16[256,2048]{1,0:T(8,128)(2,1)S(1)}, bf16[256,2048]{1,0:T(8,128)(2,1)S(1)}, u32[]{:S(2)}, u32[]{:S(2)}) collective-permute-start(bf16[256,2048]{1,0:T(8,128)(2,1)S(1)} %maximum_select_fusion.1), channel_id=1, source_target_pairs={{0,2},{1,3},{2,0},{3,1},{4,6},{5,7},{6,4},{7,5},{8,10},{9,11},{10,... | collective-permute-start | bytes 3145736 | tf_op jit(solution)/shard_map/ppermute | solution.py:28
  18.5 99.1 %collective-permute-start.1 = (bf16[1,2048,1024]{2,1,0:T(8,128)(2,1)}, bf16[1,2048,1024]{2,1,0:T(8,128)(2,1)}, u32[]{:S(2)}, u32[]{:S(2)}) collective-permute-start(bf16[1,2048,1024]{2,1,0:T(8,128)(2,1)} %param.10), channel_id=1, source_target_pairs={{28,0},{0,4},{4,8},{8,12},{12,16},{16,20},{20,24},{24,28},{29,1},{... | collective-permute-start | bytes 12582920 | tf_op jit(solution)/shard_map/ppermute | solution.py:11
  18.5 99.1 %collective-permute-start.3 = (bf16[1,2048,1024]{2,1,0:T(8,128)(2,1)}, bf16[1,2048,1024]{2,1,0:T(8,128)(2,1)}, u32[]{:S(2)}, u32[]{:S(2)}) collective-permute-start(bf16[1,2048,1024]{2,1,0:T(8,128)(2,1)} %param.10), channel_id=1, source_target_pairs={{4,0},{8,4},{12,8},{16,12},{20,16},{24,20},{28,24},{0,28},{5,1},{9... | collective-permute-start | bytes 12582920 | tf_op jit(solution)/shard_map/ppermute | solution.py:11
  41.1 5.9 %copy-start.6 = (bf16[256,2048]{1,0:T(8,128)(2,1)}, bf16[256,2048]{1,0:T(8,128)(2,1)S(1)}, u32[]{:S(2)}) copy-start(bf16[256,2048]{1,0:T(8,128)(2,1)S(1)} %collective-permute-done.5) | copy-start | bytes 3145732
  47.0 4.3 %copy-start.5 = (f32[1,4096]{1,0:T(1,128)S(1)}, f32[1,4096]{1,0:T(1,128)}, u32[]{:S(2)}) copy-start(f32[1,4096]{1,0:T(1,128)} %param.9) | copy-start | bytes 49156
  47.0 16.2 %all-to-all-start = ((bf16[4,128,1024]{2,1,0:T(8,128)(2,1)}), bf16[4,128,1024]{2,1,0:T(8,128)(2,1)S(1)}, u32[]{:S(2)}, u32[]{:S(2)}) async-start(bf16[4,128,1024]{2,1,0:T(8,128)(2,1)} %bitcast.10), calls=%async_computation | async-start | bytes 2097152 | tf_op jit(solution)/shard_map/all_to_all | solution.py:37
  63.4 1.2 copy-start.1
  63.4 1.5 %copy-start.2 = (bf16[1,128,4096]{2,1,0:T(8,128)(2,1)S(1)}, bf16[1,128,4096]{2,1,0:T(8,128)(2,1)}, u32[]{:S(2)}) copy-start(bf16[1,128,4096]{2,1,0:T(8,128)(2,1)} %param.8) | copy-start | bytes 3145732
  64.9 1.6 %copy-start = (f32[128,4,1024]{2,1,0:T(4,128)S(1)}, f32[128,4,1024]{2,1,0:T(4,128)}, u32[]{:S(2)}) copy-start(f32[128,4,1024]{2,1,0:T(4,128)} %reshape.66) | copy-start | bytes 6291460
  70.3 47.3 %copy-start.4 = (bf16[256,2048]{1,0:T(8,128)(2,1)S(1)}, bf16[256,2048]{1,0:T(8,128)(2,1)}, u32[]{:S(2)}) copy-start(bf16[256,2048]{1,0:T(8,128)(2,1)} %copy-done.3) | copy-start | bytes 3145732
  70.3 47.3 %copy-start.7 = (bf16[256,2048]{1,0:T(8,128)(2,1)S(1)}, bf16[256,2048]{1,0:T(8,128)(2,1)}, u32[]{:S(2)}) copy-start(bf16[256,2048]{1,0:T(8,128)(2,1)} %copy-done.6) | copy-start | bytes 3145732
  70.3 47.3 %all-to-all-start.1 = ((bf16[128,4,1024]{2,0,1:T(8,128)(2,1)}), bf16[128,4,1024]{2,0,1:T(8,128)(2,1)S(1)}, u32[]{:S(2)}, u32[]{:S(2)}) async-start(bf16[128,4,1024]{2,0,1:T(8,128)(2,1)} %fusion.10), calls=%async_computation.1 | async-start | bytes 2097152 | tf_op jit(solution)/shard_map/all_to_all | solution.py:43
  74.6 37.2 %collective-permute-start.2 = (bf16[1]{0:T(256)(128)(2,1)}, bf16[1]{0:T(256)(128)(2,1)}, u32[]{:S(2)}, u32[]{:S(2)}) collective-permute-start(bf16[1]{0:T(256)(128)(2,1)} %convert_element_type.66), channel_id=1, source_target_pairs={{4,0},{8,4},{12,8},{16,12},{20,16},{24,20},{28,24},{0,28},{5,1},{9... | collective-permute-start | bytes 14 | tf_op jit(solution)/shard_map/ppermute | solution.py:11
  110.8 4.9 %collective-permute-start = (bf16[1]{0:T(256)(128)(2,1)}, bf16[1]{0:T(256)(128)(2,1)}, u32[]{:S(2)}, u32[]{:S(2)}) collective-permute-start(bf16[1]{0:T(256)(128)(2,1)} %convert_element_type.66), channel_id=1, source_target_pairs={{28,0},{0,4},{4,8},{8,12},{12,16},{16,20},{20,24},{24,28},{29,1},{... | collective-permute-start | bytes 14 | tf_op jit(solution)/shard_map/ppermute | solution.py:11
